TPU v7x, 512 devices: a whole 4x8x8 slice. The times are simulated.
512 devices in a mesh: seq: 128 (over z, x_lo, y), mp: 4 (over x_hi, core).
Axes of the slice: x: 4 (x_hi: 2, x_lo: 2; x = x_hi * 2 + x_lo), y: 8, z: 8, core: 2. Of those that a mesh axis runs over, the one named last changes fastest.
Arguments:
- hidden_entry_states: bfloat16 [16384, 512], P('seq'), may hold values from -6 to 6
- base_ids: int32 [16384], P('seq'), may hold values from 0 to 4
- mask_index: int32 [2048], P('seq'), may hold values from 0 to 16383, as said below
- first_kernel: bfloat16 [9, 512, 512], P(None, None, 'mp'), may hold values from -0.09375 to 0.09375
- second_kernel: bfloat16 [9, 512, 512], P(None, None, 'mp'), may hold values from -0.09375 to 0.09375
- head_weight: bfloat16 [512, 5], replicated, may hold values from -0.5 to 0.5
Outputs:
- input_grad: bfloat16 [16384, 512], P('seq')
- first_kernel_gradient: float32 [9, 512, 512], P(None, 'seq', 'mp')
- second_kernel_gradient: float32 [9, 512, 512], P(None, 'seq', 'mp')
Inputs may be any that keep to these rules, and one draw needn't show every extreme that they name: `mask_index`: each device's 16 entries are distinct positions within its own block of 128 bases, in no particular order.
All inputs are finite; a program needn't handle non-finite values.
Results may differ from a plain program's by a relative error of at most 0.014.
Values may be sent and summed in bfloat16 or wider, within the bound.
A program may use at most 64 MiB of HBM per device.

v0:
```python
import jax
import jax.numpy as jnp
from jax import lax
from jax.sharding import PartitionSpec as P

DILATION_FIRST1 = 2048
DILATION_SECOND2 = 4096
epsilon = 1e-05
root_half = 0.7071067811865476
inv_root_two_pi = 0.3989422804014327


def shifted(x, axis, by):
    peers = lax.axis_size(axis)
    pairs = [(i, i + by) for i in range(peers) if 0 <= i + by < peers]
    return lax.ppermute(x, axis, pairs)


def gelu_parts(conv_out):
    normal_cdf = 0.5 * (1.0 + lax.erf(conv_out * root_half))
    gelu_slope = normal_cdf + conv_out * inv_root_two_pi * jnp.exp(-0.5 * conv_out * conv_out)
    return (conv_out * normal_cdf, gelu_slope)


def norm_parts(activation):
    values = activation.astype(jnp.float32)
    centre = jnp.mean(values, axis=-1, keepdims=True)
    centred = values - centre
    spread = jnp.mean(centred * centred, axis=-1, keepdims=True)
    inverse = lax.rsqrt(spread + epsilon)
    return (centred * inverse, inverse)


def loss_grad(hidden_top, targets, head_weight):
    logits = lax.dot_general(
        head_weight, hidden_top, (((0,), (1,)), ((), ())), preferred_element_type=jnp.float32
    )
    exponent = jnp.exp(logits)
    probability = exponent / jnp.sum(exponent, axis=0, keepdims=True)
    vocab_rows = lax.broadcasted_iota(jnp.int32, logits.shape, 0)
    onehot = (vocab_rows == targets[None, :]).astype(jnp.float32)
    weight = (targets >= 0).astype(jnp.float32)[None, :]
    dlogits = weight * (probability - onehot)
    return lax.dot_general(
        dlogits,
        head_weight.astype(jnp.float32),
        (((0,), (1,)), ((), ())),
        precision=lax.Precision.HIGHEST,
    )


def local(hidden_entry_states, base_ids, mask_index, first_kernel, second_kernel, head_weight):
    seq_count = lax.axis_size("seq")
    rows_per_block = hidden_entry_states.shape[0]
    channels = hidden_entry_states.shape[1]
    own_width = first_kernel.shape[2]
    tap_count = first_kernel.shape[0]
    centre_tap = tap_count // 2
    mask_count = mask_index.shape[0]
    device_row = lax.axis_index("seq")
    block_start = device_row * rows_per_block
    offsets = mask_index - block_start
    positions = lax.broadcasted_iota(jnp.int32, (rows_per_block, mask_count), 0)
    masked = jnp.any(positions == offsets[None, :], axis=1)
    targets = jnp.where(masked, base_ids, -1)

    def forward_conv(source, kernel, dilation_blocks):
        partial_value = jnp.einsum(
            "rd,kdo->kro", source, kernel, preferred_element_type=jnp.float32
        )
        summed = partial_value[centre_tap]
        for tap_index in range(tap_count):
            device_hop = dilation_blocks * (tap_index - centre_tap)
            if device_hop != 0 and abs(device_hop) < seq_count:
                summed = summed + shifted(partial_value[tap_index], "seq", -device_hop)
        return summed

    def tap_sources(grad_conv, dilation_blocks):
        pieces = []
        for tap_index in range(tap_count):
            device_hop = dilation_blocks * (tap_index - centre_tap)
            if device_hop == 0:
                pieces.append(grad_conv)
            elif abs(device_hop) >= seq_count:
                pieces.append(jnp.zeros_like(grad_conv))
            else:
                pieces.append(shifted(grad_conv, "seq", device_hop))
        return jnp.stack(pieces, axis=0)

    def block_forward_pass(source, kernel, dilation_blocks):
        conv_out = forward_conv(source, kernel, dilation_blocks)
        activation, gelu_slope = gelu_parts(conv_out)
        mixed_all = lax.all_gather(activation.astype(jnp.bfloat16), "mp", axis=1, tiled=True)
        normed, inverse = norm_parts(mixed_all)
        result = (source.astype(jnp.float32) + normed).astype(jnp.bfloat16)
        return (result, (source, normed, inverse, gelu_slope))

    def block_backward_pass(grad_out, saved, kernel, dilation_blocks):
        source, normed, inverse, gelu_slope = saved
        mean_grad = jnp.mean(grad_out, axis=-1, keepdims=True)
        mean_cross = jnp.mean(grad_out * normed, axis=-1, keepdims=True)
        grad_act = inverse * (grad_out - mean_grad - normed * mean_cross)
        own_cols = lax.dynamic_slice_in_dim(
            grad_act, lax.axis_index("mp") * own_width, own_width, 1
        )
        grad_conv = (own_cols * gelu_slope).astype(jnp.bfloat16)
        tap_stack = tap_sources(grad_conv, dilation_blocks)
        input_part = jnp.einsum(
            "kro,kdo->rd", tap_stack, kernel, preferred_element_type=jnp.float32
        )
        grad_in = grad_out + lax.psum(input_part.astype(jnp.bfloat16), "mp").astype(jnp.float32)
        kernel_part = jnp.einsum(
            "rd,kro->kdo", source, tap_stack, preferred_element_type=jnp.float32
        )
        by_owner = kernel_part.reshape(tap_count, seq_count, channels // seq_count, own_width)
        received = lax.all_to_all(
            by_owner.astype(jnp.bfloat16), "seq", split_axis=1, concat_axis=1, tiled=True
        ).astype(by_owner.dtype)
        return (grad_in, jnp.sum(received, axis=1))

    first_receptive_span = DILATION_FIRST1 // rows_per_block
    second_receptive_span = DILATION_SECOND2 // rows_per_block
    hidden_after_first, first_residuals = block_forward_pass(
        hidden_entry_states, first_kernel, first_receptive_span
    )
    hidden_after_second, second_residuals = block_forward_pass(
        hidden_after_first, second_kernel, second_receptive_span
    )
    gradient_after_second = loss_grad(hidden_after_second, targets, head_weight)
    gradient_after_first, second_kernel_gradient = block_backward_pass(
        gradient_after_second, second_residuals, second_kernel, second_receptive_span
    )
    gradient_before_first, first_kernel_gradient = block_backward_pass(
        gradient_after_first, first_residuals, first_kernel, first_receptive_span
    )
    input_grad = gradient_before_first.astype(jnp.bfloat16)
    return (input_grad, first_kernel_gradient, second_kernel_gradient)


def solution(mesh):
    placed = (P("seq", None), P("seq"), P("seq"), P(None, None, "mp"), P(None, None, "mp"), P())
    return jax.shard_map(
        local,
        mesh=mesh,
        in_specs=placed,
        out_specs=(P("seq", None), P(None, "seq", "mp"), P(None, "seq", "mp")),
        check_vma=False,
    )
```

profile of v0, /device:TPU:1, one launch (start us, length us, event | category | flops | bytes accessed | tf_op | source)
XLA Modules:
  0.0 294.8 jit_solution(10878889787662550888)
XLA Ops:
  7.2 1.9 convolution_bitcast_fusion.1
  9.2 11.5 %collective-permute-start = (f32[128,128]{0,1:T(8,128)S(1)}, f32[128,128]{0,1:T(8,128)S(1)}, u32[]{:S(2)}, u32[]{:S(2)}) collective-permute-start(f32[128,128]{0,1:T(8,128)S(1)} %get-tuple-element.30), channel_id=1, source_target_pairs={{0,256},{4,260},{8,264},{12,268},{16,272},{20,276},{24,280},{28,28... | collective-permute-start | bytes 196616 | tf_op jit(solution)/shard_map/ppermute | solution.py:16
  20.6 1.3 collective-permute-start.7
  21.9 1.3 collective-permute-start.6
  23.2 1.3 collective-permute-start.5
  24.5 1.3 collective-permute-start.4
  25.9 4.0 %collective-permute-start.3 = (f32[128,128]{0,1:T(8,128)S(1)}, f32[128,128]{0,1:T(8,128)S(1)}, u32[]{:S(2)}, u32[]{:S(2)}) collective-permute-start(f32[128,128]{0,1:T(8,128)S(1)} %get-tuple-element.35), channel_id=1, source_target_pairs={{0,64},{4,68},{8,72},{12,76},{16,80},{20,84},{24,88},{28,92},{32,9... | collective-permute-start | bytes 196616 | tf_op jit(solution)/shard_map/ppermute | solution.py:16
  29.9 0.4 collective-permute-done.7
  30.3 4.8 %collective-permute-start.2 = (f32[128,128]{0,1:T(8,128)S(1)}, f32[128,128]{0,1:T(8,128)S(1)}, u32[]{:S(2)}, u32[]{:S(2)}) collective-permute-start(f32[128,128]{0,1:T(8,128)S(1)} %get-tuple-element.36), channel_id=1, source_target_pairs={{0,128},{4,132},{8,136},{12,140},{16,144},{20,148},{24,152},{28,15... | collective-permute-start | bytes 196616 | tf_op jit(solution)/shard_map/ppermute | solution.py:16
  35.1 7.0 %collective-permute-start.1 = (f32[128,128]{0,1:T(8,128)S(1)}, f32[128,128]{0,1:T(8,128)S(1)}, u32[]{:S(2)}, u32[]{:S(2)}) collective-permute-start(f32[128,128]{0,1:T(8,128)S(1)} %get-tuple-element.37), channel_id=1, source_target_pairs={{0,192},{4,196},{8,200},{12,204},{16,208},{20,212},{24,216},{28,22... | collective-permute-start | bytes 196616 | tf_op jit(solution)/shard_map/ppermute | solution.py:16
  42.3 1.1 collective-permute-done.1
  43.4 0.7 multiply_convert_fusion.1
  44.1 9.7 %all_gather.6 = bf16[128,512]{0,1:T(8,128)(2,1)S(1)} all-gather(bf16[128,128]{0,1:T(8,128)(2,1)S(1)} %get-tuple-element.22), channel_id=1, replica_groups=mesh['seq'=128,'mp'=4] {'mp'}, dimensions={1}, use_global_device_ids=true | all-gather | bytes 163840 | tf_op jit(solution)/shard_map/all_gather | solution.py:93
  54.0 0.5 copy-done.1
  54.4 0.8 fusion.4
  55.2 0.6 convolution_bitcast_fusion
  55.8 6.9 %collective-permute-start.8 = (f32[128,128]{0,1:T(8,128)S(1)}, f32[128,128]{0,1:T(8,128)S(1)}, u32[]{:S(2)}, u32[]{:S(2)}) collective-permute-start(f32[128,128]{0,1:T(8,128)S(1)} %get-tuple-element.24), channel_id=1, source_target_pairs={{0,384},{4,388},{8,392},{12,396},{16,400},{20,404},{24,408},{28,41... | collective-permute-start | bytes 196616 | tf_op jit(solution)/shard_map/ppermute | solution.py:16
  62.9 1.3 collective-permute-start.13
  64.2 1.3 collective-permute-start.12
  65.5 1.3 collective-permute-start.11
  66.8 4.9 %collective-permute-start.10 = (f32[128,128]{0,1:T(8,128)S(1)}, f32[128,128]{0,1:T(8,128)S(1)}, u32[]{:S(2)}, u32[]{:S(2)}) collective-permute-start(f32[128,128]{0,1:T(8,128)S(1)} %get-tuple-element.28), channel_id=1, source_target_pairs={{0,128},{4,132},{8,136},{12,140},{16,144},{20,148},{24,152},{28,15... | collective-permute-start | bytes 196616 | tf_op jit(solution)/shard_map/ppermute | solution.py:16
  71.7 7.9 %collective-permute-start.9 = (f32[128,128]{0,1:T(8,128)S(1)}, f32[128,128]{0,1:T(8,128)S(1)}, u32[]{:S(2)}, u32[]{:S(2)}) collective-permute-start(f32[128,128]{0,1:T(8,128)S(1)} %get-tuple-element.29), channel_id=1, source_target_pairs={{0,256},{4,260},{8,264},{12,268},{16,272},{20,276},{24,280},{28,28... | collective-permute-start | bytes 196616 | tf_op jit(solution)/shard_map/ppermute | solution.py:16
  79.6 1.2 collective-permute-done.9
  80.9 8.9 %all_gather.7 = bf16[128,512]{0,1:T(8,128)(2,1)S(1)} all-gather(bf16[128,128]{0,1:T(8,128)(2,1)S(1)} %get-tuple-element.20), channel_id=1, replica_groups=mesh['seq'=128,'mp'=4] {'mp'}, dimensions={1}, use_global_device_ids=true | all-gather | bytes 163840 | tf_op jit(solution)/shard_map/all_gather | solution.py:93
  90.0 0.2 fusion.55
  90.2 0.4 fusion.56
  90.9 1.3 collective-permute-start.14
  92.2 6.1 %collective-permute-start.19 = (bf16[128,128]{0,1:T(8,128)(2,1)S(1)}, bf16[128,128]{0,1:T(8,128)(2,1)S(1)}, u32[]{:S(2)}, u32[]{:S(2)}) collective-permute-start(bf16[128,128]{0,1:T(8,128)(2,1)S(1)} %fusion.19), channel_id=1, source_target_pairs={{0,384},{4,388},{8,392},{12,396},{16,400},{20,404},{24,408},{28,41... | collective-permute-start | bytes 98312 | tf_op jit(solution)/shard_map/ppermute | solution.py:16
  98.3 1.8 collective-permute-start.18
  100.2 3.4 %collective-permute-start.17 = (bf16[128,128]{0,1:T(8,128)(2,1)S(1)}, bf16[128,128]{0,1:T(8,128)(2,1)S(1)}, u32[]{:S(2)}, u32[]{:S(2)}) collective-permute-start(bf16[128,128]{0,1:T(8,128)(2,1)S(1)} %fusion.19), channel_id=1, source_target_pairs={{0,128},{4,132},{8,136},{12,140},{16,144},{20,148},{24,152},{28,15... | collective-permute-start | bytes 98312 | tf_op jit(solution)/shard_map/ppermute | solution.py:16
  103.6 1.3 collective-permute-start.16
  104.9 1.3 collective-permute-start.15
  106.3 7.3 %collective-permute-done.15 = bf16[128,128]{0,1:T(8,128)(2,1)S(1)} collective-permute-done((bf16[128,128]{0,1:T(8,128)(2,1)S(1)}, bf16[128,128]{0,1:T(8,128)(2,1)S(1)}, u32[]{:S(2)}, u32[]{:S(2)}) %collective-permute-start.15) | collective-permute-done | bytes 32800 | tf_op jit(solution)/shard_map/ppermute | solution.py:16
  113.6 1.1 fusion.2
  114.8 0.5 fusion.1
  115.3 0.7 copy.68
  116.0 1.5 copy.69
  117.5 13.0 %all-to-all-start.1 = ((bf16[9,128,4,128]{3,2,0,1:T(4,128)(2,1)}), bf16[9,128,4,128]{3,2,0,1:T(4,128)(2,1)S(1)}, u32[]{:S(2)}, u32[]{:S(2)}) async-start(bf16[9,128,4,128]{3,2,0,1:T(4,128)(2,1)} %copy.69), calls=%async_computation.1 | async-start | bytes 2359296 | tf_op jit(solution)/shard_map/all_to_all | solution.py:116
  130.5 37.6 %all-reduce.3.cloned.1.call-done = bf16[128,512]{0,1:T(8,128)(2,1)} async-done(((bf16[128,512]{0,1:T(8,128)(2,1)}), bf16[128,512]{0,1:T(8,128)(2,1)}) %all-reduce.3.cloned.1.call-update) | async-done | bytes 131088 | tf_op jit(solution)/shard_map/psum | solution.py:111
  168.1 1.0 fusion.52
  169.1 0.7 copy-done.5
  169.8 0.9 fusion.24
  170.7 1.3 collective-permute-start.20
  172.0 7.9 %collective-permute-start.27 = (bf16[128,128]{0,1:T(8,128)(2,1)S(1)}, bf16[128,128]{0,1:T(8,128)(2,1)S(1)}, u32[]{:S(2)}, u32[]{:S(2)}) collective-permute-start(bf16[128,128]{0,1:T(8,128)(2,1)S(1)} %fusion.24), channel_id=1, source_target_pairs={{0,256},{4,260},{8,264},{12,268},{16,272},{20,276},{24,280},{28,28... | collective-permute-start | bytes 98312 | tf_op jit(solution)/shard_map/ppermute | solution.py:16
  179.9 5.4 %collective-permute-start.26 = (bf16[128,128]{0,1:T(8,128)(2,1)S(1)}, bf16[128,128]{0,1:T(8,128)(2,1)S(1)}, u32[]{:S(2)}, u32[]{:S(2)}) collective-permute-start(bf16[128,128]{0,1:T(8,128)(2,1)S(1)} %fusion.24), channel_id=1, source_target_pairs={{0,192},{4,196},{8,200},{12,204},{16,208},{20,212},{24,216},{28,22... | collective-permute-start | bytes 98312 | tf_op jit(solution)/shard_map/ppermute | solution.py:16
  185.2 1.3 collective-permute-start.25
  186.5 2.8 collective-permute-start.24
  189.4 1.3 collective-permute-start.21
  190.7 5.1 %collective-permute-done.21 = bf16[128,128]{0,1:T(8,128)(2,1)S(1)} collective-permute-done((bf16[128,128]{0,1:T(8,128)(2,1)S(1)}, bf16[128,128]{0,1:T(8,128)(2,1)S(1)}, u32[]{:S(2)}, u32[]{:S(2)}) %collective-permute-start.21) | collective-permute-done | bytes 32800 | tf_op jit(solution)/shard_map/ppermute | solution.py:16
  195.8 1.3 collective-permute-start.22
  197.1 4.2 %collective-permute-done.22 = bf16[128,128]{0,1:T(8,128)(2,1)S(1)} collective-permute-done((bf16[128,128]{0,1:T(8,128)(2,1)S(1)}, bf16[128,128]{0,1:T(8,128)(2,1)S(1)}, u32[]{:S(2)}, u32[]{:S(2)}) %collective-permute-start.22) | collective-permute-done | bytes 32800 | tf_op jit(solution)/shard_map/ppermute | solution.py:16
  201.4 1.3 collective-permute-start.23
  202.7 3.5 %collective-permute-done.23 = bf16[128,128]{0,1:T(8,128)(2,1)S(1)} collective-permute-done((bf16[128,128]{0,1:T(8,128)(2,1)S(1)}, bf16[128,128]{0,1:T(8,128)(2,1)S(1)}, u32[]{:S(2)}, u32[]{:S(2)}) %collective-permute-start.23) | collective-permute-done | bytes 32800 | tf_op jit(solution)/shard_map/ppermute | solution.py:16
  206.4 0.7 copy-done.6
  207.1 1.4 fusion
  208.5 1.7 copy.65
  210.2 1.4 copy.66
  211.6 11.4 %all-to-all-start = ((bf16[9,128,4,128]{3,2,0,1:T(4,128)(2,1)}), bf16[9,128,4,128]{3,2,0,1:T(4,128)(2,1)S(1)}, u32[]{:S(2)}, u32[]{:S(2)}) async-start(bf16[9,128,4,128]{3,2,0,1:T(4,128)(2,1)} %copy.66), calls=%async_computation | async-start | bytes 2359296 | tf_op jit(solution)/shard_map/all_to_all | solution.py:116
  223.1 2.5 fusion.3
  225.6 56.8 %all-reduce.5.cloned.1.call-done = bf16[128,512]{0,1:T(8,128)(2,1)} async-done(((bf16[128,512]{0,1:T(8,128)(2,1)}), bf16[128,512]{0,1:T(8,128)(2,1)}) %all-reduce.5.cloned.1.call-update) | async-done | bytes 131088 | tf_op jit(solution)/shard_map/psum | solution.py:111
  282.4 1.7 add_convert_fusion
  284.0 1.7 copy.70
  285.7 1.1 convert_reduce_fusion
  286.8 1.1 convert_reduce_fusion.1
  (89 shorter events, 1.4 us)
Async XLA Ops:
  7.2 48.0 %copy-start = (bf16[9,512,128]{2,1,0:T(8,128)(2,1)S(1)}, bf16[9,512,128]{2,1,0:T(8,128)(2,1)}, u32[]{:S(2)}) copy-start(bf16[9,512,128]{2,1,0:T(8,128)(2,1)} %param.10) | copy-start | bytes 3538948
  7.2 35.0 %copy-start.7 = (bf16[128,512]{1,0:T(8,128)(2,1)S(1)}, bf16[128,512]{1,0:T(8,128)(2,1)}, u32[]{:S(2)}) copy-start(bf16[128,512]{1,0:T(8,128)(2,1)} %param.6) | copy-start | bytes 393220
  7.2 34.9 %copy-start.12 = (s32[16]{0:T(128)S(1)}, s32[16]{0:T(128)}, u32[]{:S(2)}) copy-start(s32[16]{0:T(128)} %param.8) | copy-start | bytes 196
  7.2 160.8 %all-reduce.3.cloned.1.call-start = ((), (), s32[]{:S(2)}) async-start(), calls=%async_computation.2 | async-start | bytes 262144 | tf_op jit(solution)/shard_map/psum | solution.py:111
  9.2 16.7 %collective-permute-start = (f32[128,128]{0,1:T(8,128)S(1)}, f32[128,128]{0,1:T(8,128)S(1)}, u32[]{:S(2)}, u32[]{:S(2)}) collective-permute-start(f32[128,128]{0,1:T(8,128)S(1)} %get-tuple-element.30), channel_id=1, source_target_pairs={{0,256},{4,260},{8,264},{12,268},{16,272},{20,276},{24,280},{28,28... | collective-permute-start | bytes 196616 | tf_op jit(solution)/shard_map/ppermute | solution.py:16
  20.6 9.6 %collective-permute-start.7 = (f32[128,128]{0,1:T(8,128)S(1)}, f32[128,128]{0,1:T(8,128)S(1)}, u32[]{:S(2)}, u32[]{:S(2)}) collective-permute-start(f32[128,128]{0,1:T(8,128)S(1)} %get-tuple-element.31), channel_id=1, source_target_pairs={{256,0},{260,4},{264,8},{268,12},{272,16},{276,20},{280,24},{284,2... | collective-permute-start | bytes 196616 | tf_op jit(solution)/shard_map/ppermute | solution.py:16
  21.9 13.2 %collective-permute-start.6 = (f32[128,128]{0,1:T(8,128)S(1)}, f32[128,128]{0,1:T(8,128)S(1)}, u32[]{:S(2)}, u32[]{:S(2)}) collective-permute-start(f32[128,128]{0,1:T(8,128)S(1)} %get-tuple-element.32), channel_id=1, source_target_pairs={{192,0},{196,4},{200,8},{204,12},{208,16},{212,20},{216,24},{220,2... | collective-permute-start | bytes 196616 | tf_op jit(solution)/shard_map/ppermute | solution.py:16
  23.2 19.1 %collective-permute-start.5 = (f32[128,128]{0,1:T(8,128)S(1)}, f32[128,128]{0,1:T(8,128)S(1)}, u32[]{:S(2)}, u32[]{:S(2)}) collective-permute-start(f32[128,128]{0,1:T(8,128)S(1)} %get-tuple-element.33), channel_id=1, source_target_pairs={{128,0},{132,4},{136,8},{140,12},{144,16},{148,20},{152,24},{156,2... | collective-permute-start | bytes 196616 | tf_op jit(solution)/shard_map/ppermute | solution.py:16
  24.5 17.8 %collective-permute-start.4 = (f32[128,128]{0,1:T(8,128)S(1)}, f32[128,128]{0,1:T(8,128)S(1)}, u32[]{:S(2)}, u32[]{:S(2)}) collective-permute-start(f32[128,128]{0,1:T(8,128)S(1)} %get-tuple-element.34), channel_id=1, source_target_pairs={{64,0},{68,4},{72,8},{76,12},{80,16},{84,20},{88,24},{92,28},{96,3... | collective-permute-start | bytes 196616 | tf_op jit(solution)/shard_map/ppermute | solution.py:16
  25.9 16.5 %collective-permute-start.3 = (f32[128,128]{0,1:T(8,128)S(1)}, f32[128,128]{0,1:T(8,128)S(1)}, u32[]{:S(2)}, u32[]{:S(2)}) collective-permute-start(f32[128,128]{0,1:T(8,128)S(1)} %get-tuple-element.35), channel_id=1, source_target_pairs={{0,64},{4,68},{8,72},{12,76},{16,80},{20,84},{24,88},{28,92},{32,9... | collective-permute-start | bytes 196616 | tf_op jit(solution)/shard_map/ppermute | solution.py:16
  30.3 12.1 %collective-permute-start.2 = (f32[128,128]{0,1:T(8,128)S(1)}, f32[128,128]{0,1:T(8,128)S(1)}, u32[]{:S(2)}, u32[]{:S(2)}) collective-permute-start(f32[128,128]{0,1:T(8,128)S(1)} %get-tuple-element.36), channel_id=1, source_target_pairs={{0,128},{4,132},{8,136},{12,140},{16,144},{20,148},{24,152},{28,15... | collective-permute-start | bytes 196616 | tf_op jit(solution)/shard_map/ppermute | solution.py:16
  35.1 8.3 %collective-permute-start.1 = (f32[128,128]{0,1:T(8,128)S(1)}, f32[128,128]{0,1:T(8,128)S(1)}, u32[]{:S(2)}, u32[]{:S(2)}) collective-permute-start(f32[128,128]{0,1:T(8,128)S(1)} %get-tuple-element.37), channel_id=1, source_target_pairs={{0,192},{4,196},{8,200},{12,204},{16,208},{20,212},{24,216},{28,22... | collective-permute-start | bytes 196616 | tf_op jit(solution)/shard_map/ppermute | solution.py:16
  53.8 0.7 copy-start.1
  55.2 24.4 %copy-start.11 = (s32[128]{0:T(128)S(1)}, s32[128]{0:T(128)}, u32[]{:S(2)}) copy-start(s32[128]{0:T(128)} %param.7) | copy-start | bytes 1540
  55.8 34.2 %copy-start.10 = (bf16[512,5]{0,1:T(8,128)(2,1)S(1)}, bf16[512,5]{0,1:T(8,128)(2,1)}, u32[]{:S(2)}) copy-start(bf16[512,5]{0,1:T(8,128)(2,1)} %param.11) | copy-start | bytes 15364
  55.8 15.8 %collective-permute-start.8 = (f32[128,128]{0,1:T(8,128)S(1)}, f32[128,128]{0,1:T(8,128)S(1)}, u32[]{:S(2)}, u32[]{:S(2)}) collective-permute-start(f32[128,128]{0,1:T(8,128)S(1)} %get-tuple-element.24), channel_id=1, source_target_pairs={{0,384},{4,388},{8,392},{12,396},{16,400},{20,404},{24,408},{28,41... | collective-permute-start | bytes 196616 | tf_op jit(solution)/shard_map/ppermute | solution.py:16
  62.9 16.7 %collective-permute-start.13 = (f32[128,128]{0,1:T(8,128)S(1)}, f32[128,128]{0,1:T(8,128)S(1)}, u32[]{:S(2)}, u32[]{:S(2)}) collective-permute-start(f32[128,128]{0,1:T(8,128)S(1)} %get-tuple-element.25), channel_id=1, source_target_pairs={{384,0},{388,4},{392,8},{396,12},{400,16},{404,20},{408,24},{412,2... | collective-permute-start | bytes 196616 | tf_op jit(solution)/shard_map/ppermute | solution.py:16
  64.2 15.5 %collective-permute-start.12 = (f32[128,128]{0,1:T(8,128)S(1)}, f32[128,128]{0,1:T(8,128)S(1)}, u32[]{:S(2)}, u32[]{:S(2)}) collective-permute-start(f32[128,128]{0,1:T(8,128)S(1)} %get-tuple-element.26), channel_id=1, source_target_pairs={{256,0},{260,4},{264,8},{268,12},{272,16},{276,20},{280,24},{284,2... | collective-permute-start | bytes 196616 | tf_op jit(solution)/shard_map/ppermute | solution.py:16
  65.5 14.2 %collective-permute-start.11 = (f32[128,128]{0,1:T(8,128)S(1)}, f32[128,128]{0,1:T(8,128)S(1)}, u32[]{:S(2)}, u32[]{:S(2)}) collective-permute-start(f32[128,128]{0,1:T(8,128)S(1)} %get-tuple-element.27), channel_id=1, source_target_pairs={{128,0},{132,4},{136,8},{140,12},{144,16},{148,20},{152,24},{156,2... | collective-permute-start | bytes 196616 | tf_op jit(solution)/shard_map/ppermute | solution.py:16
  66.8 12.9 %collective-permute-start.10 = (f32[128,128]{0,1:T(8,128)S(1)}, f32[128,128]{0,1:T(8,128)S(1)}, u32[]{:S(2)}, u32[]{:S(2)}) collective-permute-start(f32[128,128]{0,1:T(8,128)S(1)} %get-tuple-element.28), channel_id=1, source_target_pairs={{0,128},{4,132},{8,136},{12,140},{16,144},{20,148},{24,152},{28,15... | collective-permute-start | bytes 196616 | tf_op jit(solution)/shard_map/ppermute | solution.py:16
  71.7 9.2 %collective-permute-start.9 = (f32[128,128]{0,1:T(8,128)S(1)}, f32[128,128]{0,1:T(8,128)S(1)}, u32[]{:S(2)}, u32[]{:S(2)}) collective-permute-start(f32[128,128]{0,1:T(8,128)S(1)} %get-tuple-element.29), channel_id=1, source_target_pairs={{0,256},{4,260},{8,264},{12,268},{16,272},{20,276},{24,280},{28,28... | collective-permute-start | bytes 196616 | tf_op jit(solution)/shard_map/ppermute | solution.py:16
  90.8 24.0 %copy-start.3 = (f32[128,512]{0,1:T(8,128)}, f32[128,512]{0,1:T(8,128)S(1)}, u32[]{:S(2)}) copy-start(f32[128,512]{0,1:T(8,128)S(1)} %copy.62) | copy-start | bytes 786436
  90.9 14.0 %collective-permute-start.14 = (bf16[128,128]{0,1:T(8,128)(2,1)S(1)}, bf16[128,128]{0,1:T(8,128)(2,1)S(1)}, u32[]{:S(2)}, u32[]{:S(2)}) collective-permute-start(bf16[128,128]{0,1:T(8,128)(2,1)S(1)} %fusion.19), channel_id=1, source_target_pairs={{384,0},{388,4},{392,8},{396,12},{400,16},{404,20},{408,24},{412,2... | collective-permute-start | bytes 98312 | tf_op jit(solution)/shard_map/ppermute | solution.py:16
  92.2 21.4 %collective-permute-start.19 = (bf16[128,128]{0,1:T(8,128)(2,1)S(1)}, bf16[128,128]{0,1:T(8,128)(2,1)S(1)}, u32[]{:S(2)}, u32[]{:S(2)}) collective-permute-start(bf16[128,128]{0,1:T(8,128)(2,1)S(1)} %fusion.19), channel_id=1, source_target_pairs={{0,384},{4,388},{8,392},{12,396},{16,400},{20,404},{24,408},{28,41... | collective-permute-start | bytes 98312 | tf_op jit(solution)/shard_map/ppermute | solution.py:16
  98.3 15.2 %collective-permute-start.18 = (bf16[128,128]{0,1:T(8,128)(2,1)S(1)}, bf16[128,128]{0,1:T(8,128)(2,1)S(1)}, u32[]{:S(2)}, u32[]{:S(2)}) collective-permute-start(bf16[128,128]{0,1:T(8,128)(2,1)S(1)} %fusion.19), channel_id=1, source_target_pairs={{0,256},{4,260},{8,264},{12,268},{16,272},{20,276},{24,280},{28,28... | collective-permute-start | bytes 98312 | tf_op jit(solution)/shard_map/ppermute | solution.py:16
  100.2 13.4 %collective-permute-start.17 = (bf16[128,128]{0,1:T(8,128)(2,1)S(1)}, bf16[128,128]{0,1:T(8,128)(2,1)S(1)}, u32[]{:S(2)}, u32[]{:S(2)}) collective-permute-start(bf16[128,128]{0,1:T(8,128)(2,1)S(1)} %fusion.19), channel_id=1, source_target_pairs={{0,128},{4,132},{8,136},{12,140},{16,144},{20,148},{24,152},{28,15... | collective-permute-start | bytes 98312 | tf_op jit(solution)/shard_map/ppermute | solution.py:16
  103.6 9.9 %collective-permute-start.16 = (bf16[128,128]{0,1:T(8,128)(2,1)S(1)}, bf16[128,128]{0,1:T(8,128)(2,1)S(1)}, u32[]{:S(2)}, u32[]{:S(2)}) collective-permute-start(bf16[128,128]{0,1:T(8,128)(2,1)S(1)} %fusion.19), channel_id=1, source_target_pairs={{128,0},{132,4},{136,8},{140,12},{144,16},{148,20},{152,24},{156,2... | collective-permute-start | bytes 98312 | tf_op jit(solution)/shard_map/ppermute | solution.py:16
  104.9 8.6 %collective-permute-start.15 = (bf16[128,128]{0,1:T(8,128)(2,1)S(1)}, bf16[128,128]{0,1:T(8,128)(2,1)S(1)}, u32[]{:S(2)}, u32[]{:S(2)}) collective-permute-start(bf16[128,128]{0,1:T(8,128)(2,1)S(1)} %fusion.19), channel_id=1, source_target_pairs={{256,0},{260,4},{264,8},{268,12},{272,16},{276,20},{280,24},{284,2... | collective-permute-start | bytes 98312 | tf_op jit(solution)/shard_map/ppermute | solution.py:16
  117.5 50.6 %copy-start.2 = (bf16[128,512]{0,1:T(8,128)(2,1)S(1)}, bf16[128,512]{0,1:T(8,128)(2,1)}, u32[]{:S(2)}) copy-start(bf16[128,512]{0,1:T(8,128)(2,1)} %copy-done.1) | copy-start | bytes 393220
  117.5 50.6 %copy-start.4 = (f32[128,512]{0,1:T(8,128)S(1)}, f32[128,512]{0,1:T(8,128)}, u32[]{:S(2)}) copy-start(f32[128,512]{0,1:T(8,128)} %copy-done.3) | copy-start | bytes 786436
  117.5 52.3 %copy-start.9 = (f32[128,128]{0,1:T(8,128)S(1)}, f32[128,128]{0,1:T(8,128)}, u32[]{:S(2)}) copy-start(f32[128,128]{0,1:T(8,128)} %get-tuple-element.23) | copy-start | bytes 196612
  117.5 94.2 %all-to-all-start.1 = ((bf16[9,128,4,128]{3,2,0,1:T(4,128)(2,1)}), bf16[9,128,4,128]{3,2,0,1:T(4,128)(2,1)S(1)}, u32[]{:S(2)}, u32[]{:S(2)}) async-start(bf16[9,128,4,128]{3,2,0,1:T(4,128)(2,1)} %copy.69), calls=%async_computation.1 | async-start | bytes 2359296 | tf_op jit(solution)/shard_map/all_to_all | solution.py:116
  130.5 76.6 %copy-start.8 = (bf16[128,512]{1,0:T(8,128)(2,1)S(1)}, bf16[128,512]{1,0:T(8,128)(2,1)}, u32[]{:S(2)}) copy-start(bf16[128,512]{1,0:T(8,128)(2,1)} %param.6) | copy-start | bytes 393220
  169.0 0.7 copy-start.5
  170.7 18.7 %collective-permute-start.20 = (bf16[128,128]{0,1:T(8,128)(2,1)S(1)}, bf16[128,128]{0,1:T(8,128)(2,1)S(1)}, u32[]{:S(2)}, u32[]{:S(2)}) collective-permute-start(bf16[128,128]{0,1:T(8,128)(2,1)S(1)} %fusion.24), channel_id=1, source_target_pairs={{256,0},{260,4},{264,8},{268,12},{272,16},{276,20},{280,24},{284,2... | collective-permute-start | bytes 98312 | tf_op jit(solution)/shard_map/ppermute | solution.py:16
  172.0 34.4 %collective-permute-start.27 = (bf16[128,128]{0,1:T(8,128)(2,1)S(1)}, bf16[128,128]{0,1:T(8,128)(2,1)S(1)}, u32[]{:S(2)}, u32[]{:S(2)}) collective-permute-start(bf16[128,128]{0,1:T(8,128)(2,1)S(1)} %fusion.24), channel_id=1, source_target_pairs={{0,256},{4,260},{8,264},{12,268},{16,272},{20,276},{24,280},{28,28... | collective-permute-start | bytes 98312 | tf_op jit(solution)/shard_map/ppermute | solution.py:16
  179.9 26.4 %collective-permute-start.26 = (bf16[128,128]{0,1:T(8,128)(2,1)S(1)}, bf16[128,128]{0,1:T(8,128)(2,1)S(1)}, u32[]{:S(2)}, u32[]{:S(2)}) collective-permute-start(bf16[128,128]{0,1:T(8,128)(2,1)S(1)} %fusion.24), channel_id=1, source_target_pairs={{0,192},{4,196},{8,200},{12,204},{16,208},{20,212},{24,216},{28,22... | collective-permute-start | bytes 98312 | tf_op jit(solution)/shard_map/ppermute | solution.py:16
  185.2 21.0 %collective-permute-start.25 = (bf16[128,128]{0,1:T(8,128)(2,1)S(1)}, bf16[128,128]{0,1:T(8,128)(2,1)S(1)}, u32[]{:S(2)}, u32[]{:S(2)}) collective-permute-start(bf16[128,128]{0,1:T(8,128)(2,1)S(1)} %fusion.24), channel_id=1, source_target_pairs={{0,128},{4,132},{8,136},{12,140},{16,144},{20,148},{24,152},{28,15... | collective-permute-start | bytes 98312 | tf_op jit(solution)/shard_map/ppermute | solution.py:16
  186.5 19.7 %collective-permute-start.24 = (bf16[128,128]{0,1:T(8,128)(2,1)S(1)}, bf16[128,128]{0,1:T(8,128)(2,1)S(1)}, u32[]{:S(2)}, u32[]{:S(2)}) collective-permute-start(bf16[128,128]{0,1:T(8,128)(2,1)S(1)} %fusion.24), channel_id=1, source_target_pairs={{0,64},{4,68},{8,72},{12,76},{16,80},{20,84},{24,88},{28,92},{32,9... | collective-permute-start | bytes 98312 | tf_op jit(solution)/shard_map/ppermute | solution.py:16
  189.4 6.5 %collective-permute-start.21 = (bf16[128,128]{0,1:T(8,128)(2,1)S(1)}, bf16[128,128]{0,1:T(8,128)(2,1)S(1)}, u32[]{:S(2)}, u32[]{:S(2)}) collective-permute-start(bf16[128,128]{0,1:T(8,128)(2,1)S(1)} %fusion.24), channel_id=1, source_target_pairs={{192,0},{196,4},{200,8},{204,12},{208,16},{212,20},{216,24},{220,2... | collective-permute-start | bytes 98312 | tf_op jit(solution)/shard_map/ppermute | solution.py:16
  195.8 5.5 %collective-permute-start.22 = (bf16[128,128]{0,1:T(8,128)(2,1)S(1)}, bf16[128,128]{0,1:T(8,128)(2,1)S(1)}, u32[]{:S(2)}, u32[]{:S(2)}) collective-permute-start(bf16[128,128]{0,1:T(8,128)(2,1)S(1)} %fusion.24), channel_id=1, source_target_pairs={{128,0},{132,4},{136,8},{140,12},{144,16},{148,20},{152,24},{156,2... | collective-permute-start | bytes 98312 | tf_op jit(solution)/shard_map/ppermute | solution.py:16
  201.4 4.9 %collective-permute-start.23 = (bf16[128,128]{0,1:T(8,128)(2,1)S(1)}, bf16[128,128]{0,1:T(8,128)(2,1)S(1)}, u32[]{:S(2)}, u32[]{:S(2)}) collective-permute-start(bf16[128,128]{0,1:T(8,128)(2,1)S(1)} %fusion.24), channel_id=1, source_target_pairs={{64,0},{68,4},{72,8},{76,12},{80,16},{84,20},{88,24},{92,28},{96,3... | collective-permute-start | bytes 98312 | tf_op jit(solution)/shard_map/ppermute | solution.py:16
  206.4 0.7 copy-start.6
  211.6 75.2 %all-to-all-start = ((bf16[9,128,4,128]{3,2,0,1:T(4,128)(2,1)}), bf16[9,128,4,128]{3,2,0,1:T(4,128)(2,1)S(1)}, u32[]{:S(2)}, u32[]{:S(2)}) async-start(bf16[9,128,4,128]{3,2,0,1:T(4,128)(2,1)} %copy.66), calls=%async_computation | async-start | bytes 2359296 | tf_op jit(solution)/shard_map/all_to_all | solution.py:116
  223.0 59.4 %all-reduce.5.cloned.1.call-start = ((), (), s32[]{:S(2)}) async-start(), calls=%async_computation.3 | async-start | bytes 262144 | tf_op jit(solution)/shard_map/psum | solution.py:111
Sparse Core Ops, SparseCore 0:
  114.9 53.0 all-reduce.2
  227.6 54.7 all-reduce.4
where the time goes:
time: 296 us; the launch traced here: 295 us
  starting transfers between devices  118 us (40%)
  waiting for transfers between devices  117 us (40%)
  blocking collectives  18.6 us (6%)
  between operations  14.7 us (5%)
  local copies, waits for them, and re-layouts  9.34 us (3%)
  matrix products  8.57 us (3%)
  other arithmetic  7.87 us (3%)
    psum x2, waiting for transfers between devices, block_backward_pass(): lax.psum(input_part.astype(jnp.bfloat16), 'mp').astype(jnp.float32)  94.4 us
    ppermute x28, starting transfers between devices, shifted(): return lax.ppermute(x, axis, pairs)  93.8 us
    all_to_all x2, starting transfers between devices, block_backward_pass(): lax.all_to_all(by_owner.astype(jnp.bfloat16), 'seq', split_axis=1, concat...  24.4 us
    ppermute x28, waiting for transfers between devices, shifted(): return lax.ppermute(x, axis, pairs)  23 us
    all_gather x2, blocking collectives, block_forward_pass(): lax.all_gather(activation.astype(jnp.bfloat16), 'mp', axis=1, tiled=True)  18.6 us
  transfers between devices with their start and end apart: 32, of which 9 were waited for; matrix products, arithmetic and copies ran while one was open for 6% of the time, Pallas kernels for 0%

commit v1 on v0

--- a/solution.py
+++ b/solution.py
@@ -113,8 +113,14 @@
             "rd,kro->kdo", source, tap_stack, preferred_element_type=jnp.float32
         )
         by_owner = kernel_part.reshape(tap_count, seq_count, channels // seq_count, own_width)
-        received = lax.all_to_all(
-            by_owner.astype(jnp.bfloat16), "seq", split_axis=1, concat_axis=1, tiled=True
+        received = jnp.concatenate(
+            lax.all_to_all(
+                jnp.stack(jnp.split(by_owner.astype(jnp.bfloat16), lax.axis_size("seq"), axis=1)),
+                "seq",
+                0,
+                0,
+            ),
+            axis=1,
         ).astype(by_owner.dtype)
         return (grad_in, jnp.sum(received, axis=1))
 

time: 296 us -> 404 us (1.36)
  local copies, waits for them, and re-layouts: 9.34 us -> 160 us
  waiting for transfers between devices: 117 us -> 67.8 us
  starting transfers between devices: 118 us -> 123 us
    unnamed x44 -> x298, local copies, waits for them, and re-layouts: 3.85 us -> 157 us
    psum x2, waiting for transfers between devices: 94.4 us -> 55.4 us  [block_backward_pass(): lax.psum(input_part.astype(jnp.bfloat16), 'mp').astype(jnp.float32)]
    ppermute x28, waiting for transfers between devices: 23 us -> 12.4 us  [shifted(): return lax.ppermute(x, axis, pairs)]
    all_to_all x2, starting transfers between devices: 24.4 us -> 28.5 us  [block_backward_pass(): lax.all_to_all(jnp.stack(jnp.split(by_owner.astype(jnp.bfloat16), lax.axi...]
  transfers between devices with their start and end apart: 32 -> 32, of which waited for: 9 -> 7; matrix products, arithmetic and copies ran while one was open for 6% -> 41% of each run, Pallas kernels for 0% -> 0%
where the time goes in v1:
time: 404 us; the launch traced here: 403 us
  local copies, waits for them, and re-layouts  160 us (40%)
  starting transfers between devices  123 us (30%)
  waiting for transfers between devices  67.8 us (17%)
  blocking collectives  19.7 us (5%)
  between operations  14.9 us (4%)
  matrix products  8.62 us (2%)
  other arithmetic  7.88 us (2%)
    unnamed x298, local copies, waits for them, and re-layouts  157 us
    ppermute x28, starting transfers between devices, shifted(): return lax.ppermute(x, axis, pairs)  94.6 us
    psum x2, waiting for transfers between devices, block_backward_pass(): lax.psum(input_part.astype(jnp.bfloat16), 'mp').astype(jnp.float32)  55.4 us
    all_to_all x2, starting transfers between devices, block_backward_pass(): lax.all_to_all(jnp.stack(jnp.split(by_owner.astype(jnp.bfloat16), lax.axi...  28.5 us
    all_gather x2, blocking collectives, block_forward_pass(): lax.all_gather(activation.astype(jnp.bfloat16), 'mp', axis=1, tiled=True)  19.7 us
    ppermute x28, waiting for transfers between devices, shifted(): return lax.ppermute(x, axis, pairs)  12.4 us
  transfers between devices with their start and end apart: 32, of which 7 were waited for; matrix products, arithmetic and copies ran while one was open for 41% of the time, Pallas kernels for 0%

profile of v1, /device:TPU:1, one launch (start us, length us, event | category | flops | bytes accessed | tf_op | source)
XLA Modules:
  0.0 402.5 jit_solution(7139814544215385090)
XLA Ops:
  7.2 1.9 convolution_bitcast_fusion.1
  9.2 1.3 collective-permute-start.7
  10.5 1.3 collective-permute-start.6
  11.8 1.3 collective-permute-start.5
  13.1 1.3 collective-permute-start.4
  14.4 5.5 %collective-permute-start.3 = (f32[128,128]{0,1:T(8,128)S(1)}, f32[128,128]{0,1:T(8,128)S(1)}, u32[]{:S(2)}, u32[]{:S(2)}) collective-permute-start(f32[128,128]{0,1:T(8,128)S(1)} %get-tuple-element.32), channel_id=1, source_target_pairs={{0,64},{4,68},{8,72},{12,76},{16,80},{20,84},{24,88},{28,92},{32,9... | collective-permute-start | bytes 196616 | tf_op jit(solution)/shard_map/ppermute | solution.py:16
  19.8 1.9 collective-permute-done.7
  21.7 5.4 %collective-permute-start.2 = (f32[128,128]{0,1:T(8,128)S(1)}, f32[128,128]{0,1:T(8,128)S(1)}, u32[]{:S(2)}, u32[]{:S(2)}) collective-permute-start(f32[128,128]{0,1:T(8,128)S(1)} %get-tuple-element.33), channel_id=1, source_target_pairs={{0,128},{4,132},{8,136},{12,140},{16,144},{20,148},{24,152},{28,15... | collective-permute-start | bytes 196616 | tf_op jit(solution)/shard_map/ppermute | solution.py:16
  27.2 7.0 %collective-permute-start.1 = (f32[128,128]{0,1:T(8,128)S(1)}, f32[128,128]{0,1:T(8,128)S(1)}, u32[]{:S(2)}, u32[]{:S(2)}) collective-permute-start(f32[128,128]{0,1:T(8,128)S(1)} %get-tuple-element.34), channel_id=1, source_target_pairs={{0,192},{4,196},{8,200},{12,204},{16,208},{20,212},{24,216},{28,22... | collective-permute-start | bytes 196616 | tf_op jit(solution)/shard_map/ppermute | solution.py:16
  34.2 3.1 collective-permute-start
  37.5 1.1 collective-permute-done
  38.6 0.7 multiply_convert_fusion.1
  39.3 12.3 %all_gather.6 = bf16[128,512]{0,1:T(8,128)(2,1)S(1)} all-gather(bf16[128,128]{0,1:T(8,128)(2,1)S(1)} %get-tuple-element.19), channel_id=1, replica_groups=mesh['seq'=128,'mp'=4] {'mp'}, dimensions={1}, use_global_device_ids=true | all-gather | bytes 163840 | tf_op jit(solution)/shard_map/all_gather | solution.py:93
  52.3 0.7 fusion.4
  53.7 1.3 collective-permute-start.13
  55.1 1.3 collective-permute-start.12
  56.3 1.3 collective-permute-start.11
  57.6 4.9 %collective-permute-start.10 = (f32[128,128]{0,1:T(8,128)S(1)}, f32[128,128]{0,1:T(8,128)S(1)}, u32[]{:S(2)}, u32[]{:S(2)}) collective-permute-start(f32[128,128]{0,1:T(8,128)S(1)} %get-tuple-element.25), channel_id=1, source_target_pairs={{0,128},{4,132},{8,136},{12,140},{16,144},{20,148},{24,152},{28,15... | collective-permute-start | bytes 196616 | tf_op jit(solution)/shard_map/ppermute | solution.py:16
  62.5 7.9 %collective-permute-start.9 = (f32[128,128]{0,1:T(8,128)S(1)}, f32[128,128]{0,1:T(8,128)S(1)}, u32[]{:S(2)}, u32[]{:S(2)}) collective-permute-start(f32[128,128]{0,1:T(8,128)S(1)} %get-tuple-element.26), channel_id=1, source_target_pairs={{0,256},{4,260},{8,264},{12,268},{16,272},{20,276},{24,280},{28,28... | collective-permute-start | bytes 196616 | tf_op jit(solution)/shard_map/ppermute | solution.py:16
  70.5 1.3 collective-permute-start.8
  71.8 3.2 collective-permute-done.8
  75.0 7.4 %all_gather.7 = bf16[128,512]{0,1:T(8,128)(2,1)S(1)} all-gather(bf16[128,128]{0,1:T(8,128)(2,1)S(1)} %get-tuple-element.17), channel_id=1, replica_groups=mesh['seq'=128,'mp'=4] {'mp'}, dimensions={1}, use_global_device_ids=true | all-gather | bytes 163840 | tf_op jit(solution)/shard_map/all_gather | solution.py:93
  83.5 1.3 collective-permute-start.14
  84.8 1.3 collective-permute-start.15
  86.1 1.3 collective-permute-start.16
  87.4 4.9 %collective-permute-start.17 = (bf16[128,128]{0,1:T(8,128)(2,1)S(1)}, bf16[128,128]{0,1:T(8,128)(2,1)S(1)}, u32[]{:S(2)}, u32[]{:S(2)}) collective-permute-start(bf16[128,128]{0,1:T(8,128)(2,1)S(1)} %fusion.19), channel_id=1, source_target_pairs={{0,128},{4,132},{8,136},{12,140},{16,144},{20,148},{24,152},{28,15... | collective-permute-start | bytes 98312 | tf_op jit(solution)/shard_map/ppermute | solution.py:16
  92.3 7.9 %collective-permute-start.18 = (bf16[128,128]{0,1:T(8,128)(2,1)S(1)}, bf16[128,128]{0,1:T(8,128)(2,1)S(1)}, u32[]{:S(2)}, u32[]{:S(2)}) collective-permute-start(bf16[128,128]{0,1:T(8,128)(2,1)S(1)} %fusion.19), channel_id=1, source_target_pairs={{0,256},{4,260},{8,264},{12,268},{16,272},{20,276},{24,280},{28,28... | collective-permute-start | bytes 98312 | tf_op jit(solution)/shard_map/ppermute | solution.py:16
  100.2 1.3 collective-permute-start.19
  101.7 0.9 collective-permute-done.19
  102.6 1.1 fusion.2
  104.2 0.7 copy.682
  127.2 0.6 constant_dynamic-update-slice_fusion.236
  144.1 0.6 constant_dynamic-update-slice_fusion.208
  146.5 0.6 constant_dynamic-update-slice_fusion.204
  159.2 0.6 constant_dynamic-update-slice_fusion.183
  181.4 1.0 fusion.52
  182.4 0.7 copy-done.5
  183.1 0.9 fusion.24
  184.0 1.3 collective-permute-start.20
  185.9 12.9 %all-to-all-start.1 = ((bf16[128,9,1,4,128]{4,3,1,2,0:T(4,128)(2,1)}), bf16[128,9,1,4,128]{4,3,1,2,0:T(4,128)(2,1)S(1)}, u32[]{:S(2)}, u32[]{:S(2)}) async-start(bf16[128,9,1,4,128]{4,3,1,2,0:T(4,128)(2,1)} %constant_dynamic-update-slice_fusion.146), calls=%async_computation.1 | async-start | bytes 2359296 | tf_op jit(solution)/shard_map/all_to_all | solution.py:117
  198.9 1.3 collective-permute-start.21
  200.2 1.3 collective-permute-start.22
  201.5 1.3 collective-permute-start.23
  202.8 4.0 collective-permute-start.24
  206.8 5.2 %collective-permute-start.25 = (bf16[128,128]{0,1:T(8,128)(2,1)S(1)}, bf16[128,128]{0,1:T(8,128)(2,1)S(1)}, u32[]{:S(2)}, u32[]{:S(2)}) collective-permute-start(bf16[128,128]{0,1:T(8,128)(2,1)S(1)} %fusion.24), channel_id=1, source_target_pairs={{0,128},{4,132},{8,136},{12,140},{16,144},{20,148},{24,152},{28,15... | collective-permute-start | bytes 98312 | tf_op jit(solution)/shard_map/ppermute | solution.py:16
  212.0 4.7 %collective-permute-done.21 = bf16[128,128]{0,1:T(8,128)(2,1)S(1)} collective-permute-done((bf16[128,128]{0,1:T(8,128)(2,1)S(1)}, bf16[128,128]{0,1:T(8,128)(2,1)S(1)}, u32[]{:S(2)}, u32[]{:S(2)}) %collective-permute-start.21) | collective-permute-done | bytes 32800 | tf_op jit(solution)/shard_map/ppermute | solution.py:16
  216.7 16.6 %collective-permute-start.26 = (bf16[128,128]{0,1:T(8,128)(2,1)S(1)}, bf16[128,128]{0,1:T(8,128)(2,1)S(1)}, u32[]{:S(2)}, u32[]{:S(2)}) collective-permute-start(bf16[128,128]{0,1:T(8,128)(2,1)S(1)} %fusion.24), channel_id=1, source_target_pairs={{0,192},{4,196},{8,200},{12,204},{16,208},{20,212},{24,216},{28,22... | collective-permute-start | bytes 98312 | tf_op jit(solution)/shard_map/ppermute | solution.py:16
  233.3 1.5 collective-permute-start.27
  234.9 0.7 collective-permute-done.27
  235.6 0.7 copy-done.6
  236.4 1.5 fusion
  237.9 1.7 copy.554
  255.2 0.6 constant_dynamic-update-slice_fusion.119
  263.0 0.6 constant_dynamic-update-slice_fusion.106
  276.8 0.6 constant_dynamic-update-slice_fusion.83
  282.9 0.6 constant_dynamic-update-slice_fusion.73
  300.3 0.6 constant_dynamic-update-slice_fusion.44
  316.6 15.6 %all-to-all-start = ((bf16[128,9,1,4,128]{4,3,1,2,0:T(4,128)(2,1)}), bf16[128,9,1,4,128]{4,3,1,2,0:T(4,128)(2,1)S(1)}, u32[]{:S(2)}, u32[]{:S(2)}) async-start(bf16[128,9,1,4,128]{4,3,1,2,0:T(4,128)(2,1)} %constant_dynamic-update-slice_fusion.18), calls=%async_computation | async-start | bytes 2359296 | tf_op jit(solution)/shard_map/all_to_all | solution.py:117
  332.3 2.5 fusion.3
  334.7 55.4 %all-reduce.5.cloned.1.call-done = bf16[128,512]{0,1:T(8,128)(2,1)} async-done(((bf16[128,512]{0,1:T(8,128)(2,1)}), bf16[128,512]{0,1:T(8,128)(2,1)}) %all-reduce.5.cloned.1.call-update) | async-done | bytes 131088 | tf_op jit(solution)/shard_map/psum | solution.py:111
  390.1 1.7 add_convert_fusion
  391.8 1.7 copy.809
  393.4 1.1 convert_reduce_fusion
  394.6 1.1 convert_reduce_fusion.1
  (343 shorter events, 152.0 us)
Async XLA Ops:
  7.2 45.9 %copy-start = (bf16[9,512,128]{2,1,0:T(8,128)(2,1)S(1)}, bf16[9,512,128]{2,1,0:T(8,128)(2,1)}, u32[]{:S(2)}) copy-start(bf16[9,512,128]{2,1,0:T(8,128)(2,1)} %param.10) | copy-start | bytes 3538948
  7.2 30.2 %copy-start.7 = (bf16[128,512]{1,0:T(8,128)(2,1)S(1)}, bf16[128,512]{1,0:T(8,128)(2,1)}, u32[]{:S(2)}) copy-start(bf16[128,512]{1,0:T(8,128)(2,1)} %param.6) | copy-start | bytes 393220
  7.2 30.1 %copy-start.12 = (s32[16]{0:T(128)S(1)}, s32[16]{0:T(128)}, u32[]{:S(2)}) copy-start(s32[16]{0:T(128)} %param.8) | copy-start | bytes 196
  7.2 174.2 %all-reduce.3.cloned.1.call-start = ((), (), s32[]{:S(2)}) async-start(), calls=%async_computation.2 | async-start | bytes 262144 | tf_op jit(solution)/shard_map/psum | solution.py:111
  9.2 12.6 %collective-permute-start.7 = (f32[128,128]{0,1:T(8,128)S(1)}, f32[128,128]{0,1:T(8,128)S(1)}, u32[]{:S(2)}, u32[]{:S(2)}) collective-permute-start(f32[128,128]{0,1:T(8,128)S(1)} %get-tuple-element.28), channel_id=1, source_target_pairs={{256,0},{260,4},{264,8},{268,12},{272,16},{276,20},{280,24},{284,2... | collective-permute-start | bytes 196616 | tf_op jit(solution)/shard_map/ppermute | solution.py:16
  10.5 16.7 %collective-permute-start.6 = (f32[128,128]{0,1:T(8,128)S(1)}, f32[128,128]{0,1:T(8,128)S(1)}, u32[]{:S(2)}, u32[]{:S(2)}) collective-permute-start(f32[128,128]{0,1:T(8,128)S(1)} %get-tuple-element.29), channel_id=1, source_target_pairs={{192,0},{196,4},{200,8},{204,12},{208,16},{212,20},{216,24},{220,2... | collective-permute-start | bytes 196616 | tf_op jit(solution)/shard_map/ppermute | solution.py:16
  11.8 22.5 %collective-permute-start.5 = (f32[128,128]{0,1:T(8,128)S(1)}, f32[128,128]{0,1:T(8,128)S(1)}, u32[]{:S(2)}, u32[]{:S(2)}) collective-permute-start(f32[128,128]{0,1:T(8,128)S(1)} %get-tuple-element.30), channel_id=1, source_target_pairs={{128,0},{132,4},{136,8},{140,12},{144,16},{148,20},{152,24},{156,2... | collective-permute-start | bytes 196616 | tf_op jit(solution)/shard_map/ppermute | solution.py:16
  13.1 24.4 %collective-permute-start.4 = (f32[128,128]{0,1:T(8,128)S(1)}, f32[128,128]{0,1:T(8,128)S(1)}, u32[]{:S(2)}, u32[]{:S(2)}) collective-permute-start(f32[128,128]{0,1:T(8,128)S(1)} %get-tuple-element.31), channel_id=1, source_target_pairs={{64,0},{68,4},{72,8},{76,12},{80,16},{84,20},{88,24},{92,28},{96,3... | collective-permute-start | bytes 196616 | tf_op jit(solution)/shard_map/ppermute | solution.py:16
  14.4 23.1 %collective-permute-start.3 = (f32[128,128]{0,1:T(8,128)S(1)}, f32[128,128]{0,1:T(8,128)S(1)}, u32[]{:S(2)}, u32[]{:S(2)}) collective-permute-start(f32[128,128]{0,1:T(8,128)S(1)} %get-tuple-element.32), channel_id=1, source_target_pairs={{0,64},{4,68},{8,72},{12,76},{16,80},{20,84},{24,88},{28,92},{32,9... | collective-permute-start | bytes 196616 | tf_op jit(solution)/shard_map/ppermute | solution.py:16
  21.7 15.8 %collective-permute-start.2 = (f32[128,128]{0,1:T(8,128)S(1)}, f32[128,128]{0,1:T(8,128)S(1)}, u32[]{:S(2)}, u32[]{:S(2)}) collective-permute-start(f32[128,128]{0,1:T(8,128)S(1)} %get-tuple-element.33), channel_id=1, source_target_pairs={{0,128},{4,132},{8,136},{12,140},{16,144},{20,148},{24,152},{28,15... | collective-permute-start | bytes 196616 | tf_op jit(solution)/shard_map/ppermute | solution.py:16
  27.2 10.3 %collective-permute-start.1 = (f32[128,128]{0,1:T(8,128)S(1)}, f32[128,128]{0,1:T(8,128)S(1)}, u32[]{:S(2)}, u32[]{:S(2)}) collective-permute-start(f32[128,128]{0,1:T(8,128)S(1)} %get-tuple-element.34), channel_id=1, source_target_pairs={{0,192},{4,196},{8,200},{12,204},{16,208},{20,212},{24,216},{28,22... | collective-permute-start | bytes 196616 | tf_op jit(solution)/shard_map/ppermute | solution.py:16
  34.2 4.4 %collective-permute-start = (f32[128,128]{0,1:T(8,128)S(1)}, f32[128,128]{0,1:T(8,128)S(1)}, u32[]{:S(2)}, u32[]{:S(2)}) collective-permute-start(f32[128,128]{0,1:T(8,128)S(1)} %get-tuple-element.27), channel_id=1, source_target_pairs={{0,256},{4,260},{8,264},{12,268},{16,272},{20,276},{24,280},{28,28... | collective-permute-start | bytes 196616 | tf_op jit(solution)/shard_map/ppermute | solution.py:16
  51.6 0.7 copy-start.1
  53.0 18.7 %copy-start.11 = (s32[128]{0:T(128)S(1)}, s32[128]{0:T(128)}, u32[]{:S(2)}) copy-start(s32[128]{0:T(128)} %param.7) | copy-start | bytes 1540
  53.6 29.0 %copy-start.10 = (bf16[512,5]{0,1:T(8,128)(2,1)S(1)}, bf16[512,5]{0,1:T(8,128)(2,1)}, u32[]{:S(2)}) copy-start(bf16[512,5]{0,1:T(8,128)(2,1)} %param.11) | copy-start | bytes 15364
  53.7 16.8 %collective-permute-start.13 = (f32[128,128]{0,1:T(8,128)S(1)}, f32[128,128]{0,1:T(8,128)S(1)}, u32[]{:S(2)}, u32[]{:S(2)}) collective-permute-start(f32[128,128]{0,1:T(8,128)S(1)} %get-tuple-element.22), channel_id=1, source_target_pairs={{384,0},{388,4},{392,8},{396,12},{400,16},{404,20},{408,24},{412,2... | collective-permute-start | bytes 196616 | tf_op jit(solution)/shard_map/ppermute | solution.py:16
  55.1 16.7 %collective-permute-start.12 = (f32[128,128]{0,1:T(8,128)S(1)}, f32[128,128]{0,1:T(8,128)S(1)}, u32[]{:S(2)}, u32[]{:S(2)}) collective-permute-start(f32[128,128]{0,1:T(8,128)S(1)} %get-tuple-element.23), channel_id=1, source_target_pairs={{256,0},{260,4},{264,8},{268,12},{272,16},{276,20},{280,24},{284,2... | collective-permute-start | bytes 196616 | tf_op jit(solution)/shard_map/ppermute | solution.py:16
  56.3 15.5 %collective-permute-start.11 = (f32[128,128]{0,1:T(8,128)S(1)}, f32[128,128]{0,1:T(8,128)S(1)}, u32[]{:S(2)}, u32[]{:S(2)}) collective-permute-start(f32[128,128]{0,1:T(8,128)S(1)} %get-tuple-element.24), channel_id=1, source_target_pairs={{128,0},{132,4},{136,8},{140,12},{144,16},{148,20},{152,24},{156,2... | collective-permute-start | bytes 196616 | tf_op jit(solution)/shard_map/ppermute | solution.py:16
  57.6 14.2 %collective-permute-start.10 = (f32[128,128]{0,1:T(8,128)S(1)}, f32[128,128]{0,1:T(8,128)S(1)}, u32[]{:S(2)}, u32[]{:S(2)}) collective-permute-start(f32[128,128]{0,1:T(8,128)S(1)} %get-tuple-element.25), channel_id=1, source_target_pairs={{0,128},{4,132},{8,136},{12,140},{16,144},{20,148},{24,152},{28,15... | collective-permute-start | bytes 196616 | tf_op jit(solution)/shard_map/ppermute | solution.py:16
  62.5 9.3 %collective-permute-start.9 = (f32[128,128]{0,1:T(8,128)S(1)}, f32[128,128]{0,1:T(8,128)S(1)}, u32[]{:S(2)}, u32[]{:S(2)}) collective-permute-start(f32[128,128]{0,1:T(8,128)S(1)} %get-tuple-element.26), channel_id=1, source_target_pairs={{0,256},{4,260},{8,264},{12,268},{16,272},{20,276},{24,280},{28,28... | collective-permute-start | bytes 196616 | tf_op jit(solution)/shard_map/ppermute | solution.py:16
  70.5 4.5 %collective-permute-start.8 = (f32[128,128]{0,1:T(8,128)S(1)}, f32[128,128]{0,1:T(8,128)S(1)}, u32[]{:S(2)}, u32[]{:S(2)}) collective-permute-start(f32[128,128]{0,1:T(8,128)S(1)} %get-tuple-element.21), channel_id=1, source_target_pairs={{0,384},{4,388},{8,392},{12,396},{16,400},{20,404},{24,408},{28,41... | collective-permute-start | bytes 196616 | tf_op jit(solution)/shard_map/ppermute | solution.py:16
  83.4 20.3 %copy-start.3 = (f32[128,512]{0,1:T(8,128)}, f32[128,512]{0,1:T(8,128)S(1)}, u32[]{:S(2)}) copy-start(f32[128,512]{0,1:T(8,128)S(1)} %copy.551) | copy-start | bytes 786436
  83.5 16.7 %collective-permute-start.14 = (bf16[128,128]{0,1:T(8,128)(2,1)S(1)}, bf16[128,128]{0,1:T(8,128)(2,1)S(1)}, u32[]{:S(2)}, u32[]{:S(2)}) collective-permute-start(bf16[128,128]{0,1:T(8,128)(2,1)S(1)} %fusion.19), channel_id=1, source_target_pairs={{384,0},{388,4},{392,8},{396,12},{400,16},{404,20},{408,24},{412,2... | collective-permute-start | bytes 98312 | tf_op jit(solution)/shard_map/ppermute | solution.py:16
  84.8 16.7 %collective-permute-start.15 = (bf16[128,128]{0,1:T(8,128)(2,1)S(1)}, bf16[128,128]{0,1:T(8,128)(2,1)S(1)}, u32[]{:S(2)}, u32[]{:S(2)}) collective-permute-start(bf16[128,128]{0,1:T(8,128)(2,1)S(1)} %fusion.19), channel_id=1, source_target_pairs={{256,0},{260,4},{264,8},{268,12},{272,16},{276,20},{280,24},{284,2... | collective-permute-start | bytes 98312 | tf_op jit(solution)/shard_map/ppermute | solution.py:16
  86.1 15.4 %collective-permute-start.16 = (bf16[128,128]{0,1:T(8,128)(2,1)S(1)}, bf16[128,128]{0,1:T(8,128)(2,1)S(1)}, u32[]{:S(2)}, u32[]{:S(2)}) collective-permute-start(bf16[128,128]{0,1:T(8,128)(2,1)S(1)} %fusion.19), channel_id=1, source_target_pairs={{128,0},{132,4},{136,8},{140,12},{144,16},{148,20},{152,24},{156,2... | collective-permute-start | bytes 98312 | tf_op jit(solution)/shard_map/ppermute | solution.py:16
  87.4 14.2 %collective-permute-start.17 = (bf16[128,128]{0,1:T(8,128)(2,1)S(1)}, bf16[128,128]{0,1:T(8,128)(2,1)S(1)}, u32[]{:S(2)}, u32[]{:S(2)}) collective-permute-start(bf16[128,128]{0,1:T(8,128)(2,1)S(1)} %fusion.19), channel_id=1, source_target_pairs={{0,128},{4,132},{8,136},{12,140},{16,144},{20,148},{24,152},{28,15... | collective-permute-start | bytes 98312 | tf_op jit(solution)/shard_map/ppermute | solution.py:16
  92.3 9.3 %collective-permute-start.18 = (bf16[128,128]{0,1:T(8,128)(2,1)S(1)}, bf16[128,128]{0,1:T(8,128)(2,1)S(1)}, u32[]{:S(2)}, u32[]{:S(2)}) collective-permute-start(bf16[128,128]{0,1:T(8,128)(2,1)S(1)} %fusion.19), channel_id=1, source_target_pairs={{0,256},{4,260},{8,264},{12,268},{16,272},{20,276},{24,280},{28,28... | collective-permute-start | bytes 98312 | tf_op jit(solution)/shard_map/ppermute | solution.py:16
  100.2 2.3 collective-permute-start.19
  104.9 76.5 %copy-start.2 = (bf16[128,512]{0,1:T(8,128)(2,1)S(1)}, bf16[128,512]{0,1:T(8,128)(2,1)}, u32[]{:S(2)}) copy-start(bf16[128,512]{0,1:T(8,128)(2,1)} %copy-done.1) | copy-start | bytes 393220
  104.9 76.5 %copy-start.4 = (f32[128,512]{0,1:T(8,128)S(1)}, f32[128,512]{0,1:T(8,128)}, u32[]{:S(2)}) copy-start(f32[128,512]{0,1:T(8,128)} %copy-done.3) | copy-start | bytes 786436
  130.8 52.3 %copy-start.9 = (f32[128,128]{0,1:T(8,128)S(1)}, f32[128,128]{0,1:T(8,128)}, u32[]{:S(2)}) copy-start(f32[128,128]{0,1:T(8,128)} %get-tuple-element.20) | copy-start | bytes 196612
  182.4 0.7 copy-start.5
  184.0 22.7 %collective-permute-start.20 = (bf16[128,128]{0,1:T(8,128)(2,1)S(1)}, bf16[128,128]{0,1:T(8,128)(2,1)S(1)}, u32[]{:S(2)}, u32[]{:S(2)}) collective-permute-start(bf16[128,128]{0,1:T(8,128)(2,1)S(1)} %fusion.24), channel_id=1, source_target_pairs={{256,0},{260,4},{264,8},{268,12},{272,16},{276,20},{280,24},{284,2... | collective-permute-start | bytes 98312 | tf_op jit(solution)/shard_map/ppermute | solution.py:16
  185.9 50.4 %copy-start.8 = (bf16[128,512]{1,0:T(8,128)(2,1)S(1)}, bf16[128,512]{1,0:T(8,128)(2,1)}, u32[]{:S(2)}) copy-start(bf16[128,512]{1,0:T(8,128)(2,1)} %param.6) | copy-start | bytes 393220
  185.9 130.7 %all-to-all-start.1 = ((bf16[128,9,1,4,128]{4,3,1,2,0:T(4,128)(2,1)}), bf16[128,9,1,4,128]{4,3,1,2,0:T(4,128)(2,1)S(1)}, u32[]{:S(2)}, u32[]{:S(2)}) async-start(bf16[128,9,1,4,128]{4,3,1,2,0:T(4,128)(2,1)} %constant_dynamic-update-slice_fusion.146), calls=%async_computation.1 | async-start | bytes 2359296 | tf_op jit(solution)/shard_map/all_to_all | solution.py:117
  198.9 17.8 %collective-permute-start.21 = (bf16[128,128]{0,1:T(8,128)(2,1)S(1)}, bf16[128,128]{0,1:T(8,128)(2,1)S(1)}, u32[]{:S(2)}, u32[]{:S(2)}) collective-permute-start(bf16[128,128]{0,1:T(8,128)(2,1)S(1)} %fusion.24), channel_id=1, source_target_pairs={{192,0},{196,4},{200,8},{204,12},{208,16},{212,20},{216,24},{220,2... | collective-permute-start | bytes 98312 | tf_op jit(solution)/shard_map/ppermute | solution.py:16
  200.2 33.1 %collective-permute-start.22 = (bf16[128,128]{0,1:T(8,128)(2,1)S(1)}, bf16[128,128]{0,1:T(8,128)(2,1)S(1)}, u32[]{:S(2)}, u32[]{:S(2)}) collective-permute-start(bf16[128,128]{0,1:T(8,128)(2,1)S(1)} %fusion.24), channel_id=1, source_target_pairs={{128,0},{132,4},{136,8},{140,12},{144,16},{148,20},{152,24},{156,2... | collective-permute-start | bytes 98312 | tf_op jit(solution)/shard_map/ppermute | solution.py:16
  201.5 33.4 %collective-permute-start.23 = (bf16[128,128]{0,1:T(8,128)(2,1)S(1)}, bf16[128,128]{0,1:T(8,128)(2,1)S(1)}, u32[]{:S(2)}, u32[]{:S(2)}) collective-permute-start(bf16[128,128]{0,1:T(8,128)(2,1)S(1)} %fusion.24), channel_id=1, source_target_pairs={{64,0},{68,4},{72,8},{76,12},{80,16},{84,20},{88,24},{92,28},{96,3... | collective-permute-start | bytes 98312 | tf_op jit(solution)/shard_map/ppermute | solution.py:16
  202.8 32.1 %collective-permute-start.24 = (bf16[128,128]{0,1:T(8,128)(2,1)S(1)}, bf16[128,128]{0,1:T(8,128)(2,1)S(1)}, u32[]{:S(2)}, u32[]{:S(2)}) collective-permute-start(bf16[128,128]{0,1:T(8,128)(2,1)S(1)} %fusion.24), channel_id=1, source_target_pairs={{0,64},{4,68},{8,72},{12,76},{16,80},{20,84},{24,88},{28,92},{32,9... | collective-permute-start | bytes 98312 | tf_op jit(solution)/shard_map/ppermute | solution.py:16
  206.8 28.1 %collective-permute-start.25 = (bf16[128,128]{0,1:T(8,128)(2,1)S(1)}, bf16[128,128]{0,1:T(8,128)(2,1)S(1)}, u32[]{:S(2)}, u32[]{:S(2)}) collective-permute-start(bf16[128,128]{0,1:T(8,128)(2,1)S(1)} %fusion.24), channel_id=1, source_target_pairs={{0,128},{4,132},{8,136},{12,140},{16,144},{20,148},{24,152},{28,15... | collective-permute-start | bytes 98312 | tf_op jit(solution)/shard_map/ppermute | solution.py:16
  216.7 18.2 %collective-permute-start.26 = (bf16[128,128]{0,1:T(8,128)(2,1)S(1)}, bf16[128,128]{0,1:T(8,128)(2,1)S(1)}, u32[]{:S(2)}, u32[]{:S(2)}) collective-permute-start(bf16[128,128]{0,1:T(8,128)(2,1)S(1)} %fusion.24), channel_id=1, source_target_pairs={{0,192},{4,196},{8,200},{12,204},{16,208},{20,212},{24,216},{28,22... | collective-permute-start | bytes 98312 | tf_op jit(solution)/shard_map/ppermute | solution.py:16
  233.3 2.3 collective-permute-start.27
  235.6 0.7 copy-start.6
  316.6 78.0 %all-to-all-start = ((bf16[128,9,1,4,128]{4,3,1,2,0:T(4,128)(2,1)}), bf16[128,9,1,4,128]{4,3,1,2,0:T(4,128)(2,1)S(1)}, u32[]{:S(2)}, u32[]{:S(2)}) async-start(bf16[128,9,1,4,128]{4,3,1,2,0:T(4,128)(2,1)} %constant_dynamic-update-slice_fusion.18), calls=%async_computation | async-start | bytes 2359296 | tf_op jit(solution)/shard_map/all_to_all | solution.py:117
  332.2 57.9 %all-reduce.5.cloned.1.call-start = ((), (), s32[]{:S(2)}) async-start(), calls=%async_computation.3 | async-start | bytes 262144 | tf_op jit(solution)/shard_map/psum | solution.py:111
Sparse Core Ops, SparseCore 0:
  104.3 50.1 all-reduce.2
  336.8 53.2 all-reduce.4
